TPU v7x, 32 devices: a whole 2x2x4 slice. The times are simulated.
32 devices in a mesh: gy: 8 (over z, x), gx: 4 (over y, core).
Axes of the slice: x: 2, y: 2, z: 4, core: 2. Of those that a mesh axis runs over, the one named last changes fastest.
Arguments:
- cell_index: int32 [3, 12288], P(None, ('gy', 'gx')), may hold values from 0 to 383, as said below
- offsets: float32 [3, 12288], P(None, ('gy', 'gx')), may hold values from 0 to 1
- charges: float32 [12288], P(('gy', 'gx')), may hold values from -6 to 6
- dipoles: float32 [3, 12288], P(None, ('gy', 'gx')), may hold values from -6 to 6
- block_count: int32 [192], P(('gy', 'gx')), may hold values from 32 to 64, as said below
- shear_cells: int32 [1], replicated, may hold values from 1 to 383
Outputs:
- charge_grad: float32 [12288], P(('gy', 'gx'))
- dipole_grad: float32 [3, 12288], P(None, ('gy', 'gx'))
- position_grad: float32 [3, 12288], P(None, ('gy', 'gx'))
- energy: float32 [1], replicated
Inputs may be any that keep to these rules, and one draw needn't show every extreme that they name: `cell_index`: slot s lies in block k = s // 64; block k lies on the device d = k // 6 at gy index d // 4 and gx index d % 4; its atoms have x cells from (d % 4) * 96 + (k % 6) * 16 up to 15 beyond, y cells from (d // 4) * 6 up to 5 beyond, and z cells below 360. The first slot of each block sits at the largest x, y and z cells of that range. Row 0 holds x, row 1 y, row 2 z. The live atoms of a block are its first block_count slots; every device holds a full block.
All inputs are finite; a program needn't handle non-finite values.
Results may differ from a plain program's by a relative error of at most 0.0003.
Values sent between devices are 32-bit elements; how exact they have to be, the bound alone decides.
A program may use at most 128 MiB of HBM per device.

v0:
```python
import math

import jax
import jax.numpy as jnp
from jax import lax
from jax.sharding import PartitionSpec as P

NX = 384
NZ = 360
CY = 6
BX = 16


screening = 0.9
combos = (
    (0, 0, 0),
    (1, 0, 0),
    (0, 1, 0),
    (0, 0, 1),
    (2, 0, 0),
    (0, 2, 0),
    (0, 0, 2),
    (1, 1, 0),
    (1, 0, 1),
    (0, 1, 1),
)
planar_orders = ((0, 0), (1, 0), (0, 1), (2, 0), (0, 2), (1, 1))


def spline_tables(fraction):
    levels = {2: [1.0 - fraction, fraction]}
    current = levels[2]
    for n in range(3, 7):
        inverse_n = 1.0 / (n - 1)
        updated = [None] * n
        updated[n - 1] = inverse_n * fraction * current[n - 2]
        for j in range(1, n - 1):
            updated[n - 1 - j] = inverse_n * (
                (fraction + j) * current[n - 2 - j] + (n - j - fraction) * current[n - 1 - j]
            )
        updated[0] = inverse_n * (1.0 - fraction) * current[0]
        current = updated
        levels[n] = current
    zero_row = jnp.zeros_like(fraction)

    def entry_at(values_list, k):
        return values_list[k] if 0 <= k < len(values_list) else zero_row

    values_w = jnp.stack(levels[6])
    first_w = jnp.stack([entry_at(levels[5], t - 1) - entry_at(levels[5], t) for t in range(6)])
    second_w = jnp.stack(
        [
            entry_at(levels[4], t - 2) - 2.0 * entry_at(levels[4], t - 1) + entry_at(levels[4], t)
            for t in range(6)
        ]
    )
    return jnp.stack([values_w, first_w, second_w])


def spline_modulus(angles):
    return (66.0 + 52.0 * jnp.cos(angles) + 2.0 * jnp.cos(2.0 * angles)) / 120.0


def green_values(index_x, index_y, index_z, shear_step, size_x, size_y, size_z):
    fold_x = (index_x + size_x // 2) % size_x - size_x // 2
    fold_y = (index_y + size_y // 2) % size_y - size_y // 2
    fold_z = (index_z + size_z // 2) % size_z - size_z // 2
    float_x = fold_x.astype(jnp.float32)
    float_z = fold_z.astype(jnp.float32)
    wave_y = fold_y.astype(jnp.float32) + float_x * shear_step.astype(jnp.float32) / size_x
    square_norm = (float_x / size_x) ** 2 + (wave_y / size_y) ** 2 + (float_z / size_z) ** 2
    is_zero = (fold_x == 0) & (fold_y == 0) & (fold_z == 0)
    at_edge = (fold_x == -(size_x // 2)) | (fold_y == -(size_y // 2)) | (fold_z == -(size_z // 2))
    safe_norm = jnp.where(is_zero, 1.0, square_norm)
    moduli = (
        spline_modulus(2.0 * math.pi * float_x / size_x)
        * spline_modulus(2.0 * math.pi * wave_y / size_y)
        * spline_modulus(2.0 * math.pi * float_z / size_z)
    )
    kernel = jnp.exp(-((math.pi / screening) ** 2) * safe_norm) / (
        math.pi * safe_norm * moduli * moduli
    )
    return jnp.where(is_zero | at_edge, 0.0, kernel)


def dense_weights(tables, base_cell, length, period):
    columns = jnp.arange(length, dtype=jnp.int32)
    summed = jnp.zeros((3, base_cell.shape[0], length), jnp.float32)
    for t in range(6):
        position = base_cell + t
        if period > 0:
            position = position % period
        matches = (position[:, None] == columns[None, :]).astype(jnp.float32)
        summed = summed + tables[:, t, :, None] * matches[None, :, :]
    return summed


def twiddle(rows_index, cols_index, period):
    tick_count = rows_index[:, None] * cols_index[None, :] % period
    angles = 2.0 * math.pi / period * tick_count.astype(jnp.float32)
    return (jnp.cos(angles), jnp.sin(angles))


def contract(pattern, operand, matrix):
    return jnp.einsum(pattern, operand, matrix, precision=lax.Precision.HIGHEST)


def forward_pair(pattern, real_in, imag_in, cos_table, sin_table):
    real_out = contract(pattern, real_in, cos_table) + contract(pattern, imag_in, sin_table)
    imag_out = contract(pattern, imag_in, cos_table) - contract(pattern, real_in, sin_table)
    return (real_out, imag_out)


def inverse_pair(pattern, real_in, imag_in, cos_table, sin_table):
    real_out = contract(pattern, real_in, cos_table) - contract(pattern, imag_in, sin_table)
    imag_out = contract(pattern, imag_in, cos_table) + contract(pattern, real_in, sin_table)
    return (real_out, imag_out)


def on_device(cell_index, offsets, charges, dipoles, block_count, shear_cells):
    groups_x = lax.axis_size("gx")
    groups_y = lax.axis_size("gy")
    pencil_index = lax.axis_index("gx")
    slab_index = lax.axis_index("gy")
    width_x = NX // groups_x
    window_x = width_x + 5
    depth_y = CY + 5
    block_x = BX + 5
    total_y = CY * groups_y
    part_x = NX // groups_y
    blocks = block_count.shape[0]
    per_block = charges.shape[0] // blocks
    shear_step = shear_cells[0]
    slot_rank = jnp.arange(per_block, dtype=jnp.int32)
    spread_grid = jnp.zeros((depth_y, window_x, NZ), jnp.float32)
    block_store = []
    for b in range(blocks):
        first_slot = b * per_block
        last_slot = first_slot + per_block
        live_slots = (slot_rank < block_count[b]).astype(jnp.float32)
        charge_live = charges[first_slot:last_slot] * live_slots
        dipole_live = dipoles[:, first_slot:last_slot] * live_slots[None, :]
        local_x = cell_index[0, first_slot:last_slot] - pencil_index * width_x - b * BX
        local_y = cell_index[1, first_slot:last_slot] - slab_index * CY
        dense_x = dense_weights(
            spline_tables(offsets[0, first_slot:last_slot]), local_x, block_x, 0
        )
        dense_y = dense_weights(
            spline_tables(offsets[1, first_slot:last_slot]), local_y, depth_y, 0
        )
        dense_z = dense_weights(
            spline_tables(offsets[2, first_slot:last_slot]),
            cell_index[2, first_slot:last_slot],
            NZ,
            NZ,
        )
        planar = {}
        for p, r in planar_orders:
            planar[p, r] = (dense_y[r][:, :, None] * dense_x[p][:, None, :]).reshape(
                per_block, depth_y * block_x
            )
        left_side = jnp.concatenate(
            [
                planar[0, 0],
                dipole_live[0][:, None] * planar[1, 0] + dipole_live[1][:, None] * planar[0, 1],
            ],
            axis=0,
        )
        right_side = jnp.concatenate(
            [charge_live[:, None] * dense_z[0] + dipole_live[2][:, None] * dense_z[1], dense_z[0]],
            axis=0,
        )
        block_grid = contract("ac,az->cz", left_side, right_side).reshape(depth_y, block_x, NZ)
        spread_grid = spread_grid.at[:, b * BX : b * BX + block_x, :].add(block_grid)
        block_store.append((planar, dense_z, live_slots, charge_live, dipole_live))
    rows_z = jnp.arange(NZ, dtype=jnp.int32)
    kept_z = NZ
    modes_z = jnp.arange(kept_z, dtype=jnp.int32)
    fold_weight = jnp.ones((kept_z,), jnp.float32)
    part_z = kept_z // groups_x
    cos_z, sin_z = twiddle(rows_z, modes_z, NZ)
    back_cos = cos_z * fold_weight[None, :]
    back_sin = sin_z * fold_weight[None, :]
    real_part = contract("yxz,zk->ykx", spread_grid, cos_z)
    imag_part = -contract("yxz,zk->ykx", spread_grid, sin_z)
    pencils = lax.all_to_all(
        jnp.stack([real_part, imag_part]), "gx", split_axis=2, concat_axis=3, tiled=True
    )
    extended = jnp.arange(groups_x * window_x, dtype=jnp.int32)
    place_x = extended // window_x * width_x + extended % window_x
    modes_x = jnp.arange(NX, dtype=jnp.int32)
    cos_x, sin_x = twiddle(place_x, modes_x, NX)
    real_part, imag_part = forward_pair("ykx,xm->ykm", pencils[0], pencils[1], cos_x, sin_x)
    fold_x = (modes_x + NX // 2) % NX - NX // 2
    rows_y = slab_index * CY + jnp.arange(depth_y, dtype=jnp.int32)
    tick_count = rows_y[:, None] * shear_step * fold_x[None, :] % (NX * total_y)
    angles = 2.0 * math.pi / (NX * total_y) * tick_count.astype(jnp.float32)
    cos_t = jnp.cos(angles)[:, None, :]
    sin_t = jnp.sin(angles)[:, None, :]
    twisted = jnp.stack(
        [real_part * cos_t + imag_part * sin_t, imag_part * cos_t - real_part * sin_t]
    )
    gathered = lax.all_to_all(twisted, "gy", split_axis=3, concat_axis=1, tiled=True)
    ext_y = jnp.arange(groups_y * depth_y, dtype=jnp.int32)
    place_y = ext_y // depth_y * CY + ext_y % depth_y
    modes_y = jnp.arange(total_y, dtype=jnp.int32)
    cos_y, sin_y = twiddle(place_y, modes_y, total_y)
    spectrum_real, spectrum_imag = forward_pair(
        "yzm,yn->nzm", gathered[0], gathered[1], cos_y, sin_y
    )
    index_z = pencil_index * part_z + jnp.arange(part_z, dtype=jnp.int32)
    index_x = slab_index * part_x + jnp.arange(part_x, dtype=jnp.int32)
    green_k = green_values(
        index_x[None, None, :],
        modes_y[:, None, None],
        index_z[None, :, None],
        shear_step,
        NX,
        total_y,
        NZ,
    )
    own_weight = lax.dynamic_slice_in_dim(fold_weight, pencil_index * part_z, part_z)
    local_energy = (
        0.5
        / (NX * total_y * NZ)
        * jnp.sum(
            green_k
            * own_weight[None, :, None]
            * (spectrum_real * spectrum_real + spectrum_imag * spectrum_imag)
        )
    )
    energy = lax.psum(local_energy, ("gy", "gx"))
    scaled = green_k / (NX * total_y * NZ)
    back_real, back_imag = inverse_pair(
        "nzm,yn->yzm", scaled * spectrum_real, scaled * spectrum_imag, cos_y, sin_y
    )
    returned = lax.all_to_all(
        jnp.stack([back_real, back_imag]), "gy", split_axis=1, concat_axis=3, tiled=True
    )
    plain_real = returned[0] * cos_t - returned[1] * sin_t
    plain_imag = returned[1] * cos_t + returned[0] * sin_t
    line_real, line_imag = inverse_pair("ykm,xm->ykx", plain_real, plain_imag, cos_x, sin_x)
    arrived_x = lax.all_to_all(
        jnp.stack([line_real, line_imag]), "gx", split_axis=3, concat_axis=2, tiled=True
    )
    potential = contract("ykx,zk->yxz", arrived_x[0], back_cos) - contract(
        "ykx,zk->yxz", arrived_x[1], back_sin
    )
    charge_parts = []
    dipole_parts = []
    position_parts = []
    atom_energy = jnp.zeros((), jnp.float32)
    for b in range(blocks):
        planar, dense_z, live_slots, charge_live, dipole_live = block_store[b]
        window_cells = potential[:, b * BX : b * BX + block_x, :].reshape(depth_y * block_x, NZ)
        projected = contract("cz,daz->dac", window_cells, dense_z)
        sampled = [jnp.sum(planar[p, r] * projected[s], axis=1) for p, r, s in combos]
        field = jnp.stack(sampled[1:4])
        charge_parts.append(live_slots * sampled[0])
        dipole_parts.append(live_slots[None, :] * field)
        force_x = (
            charge_live * sampled[1]
            + dipole_live[0] * sampled[4]
            + dipole_live[1] * sampled[7]
            + dipole_live[2] * sampled[8]
        )
        force_y = (
            charge_live * sampled[2]
            + dipole_live[0] * sampled[7]
            + dipole_live[1] * sampled[5]
            + dipole_live[2] * sampled[9]
        )
        force_z = (
            charge_live * sampled[3]
            + dipole_live[0] * sampled[8]
            + dipole_live[1] * sampled[9]
            + dipole_live[2] * sampled[6]
        )
        position_parts.append(live_slots[None, :] * jnp.stack([force_x, force_y, force_z]))
        atom_energy = atom_energy + 0.5 * jnp.sum(
            charge_live * sampled[0] + jnp.sum(dipole_live * field, axis=0)
        )
    charge_grad = jnp.concatenate(charge_parts, axis=0)
    dipole_grad = jnp.concatenate(dipole_parts, axis=1)
    position_grad = jnp.concatenate(position_parts, axis=1)
    return (charge_grad, dipole_grad, position_grad, jnp.reshape(energy, (1,)))


def solution(mesh):
    placed = (
        P(None, ("gy", "gx")),
        P(None, ("gy", "gx")),
        P(("gy", "gx")),
        P(None, ("gy", "gx")),
        P(("gy", "gx")),
        P(),
    )
    return jax.shard_map(
        on_device,
        mesh=mesh,
        in_specs=placed,
        out_specs=(P(("gy", "gx")), P(None, ("gy", "gx")), P(None, ("gy", "gx")), P()),
        check_vma=False,
    )
```

profile of v0, /device:TPU:0, one launch (start us, length us, event | category | flops | bytes accessed | tf_op | source)
XLA Modules:
  0.0 631.9 jit_solution(13073522731978985152)
XLA Ops:
  1.5 1.0 broadcast_add_fusion.31
  7.4 1.0 add_multiply_fusion.12
  9.9 1.0 add_multiply_fusion.13
  14.3 1.0 add_multiply_fusion.15
  20.3 1.6 fusion.494
  25.8 5.4 slice_select_fusion
  51.2 1.5 broadcast_multiply_fusion.8
  60.4 5.2 scatter-add.21
  65.6 4.8 scatter-add.24
  70.5 4.8 scatter-add.25
  75.3 4.3 scatter-add.26
  79.7 5.9 negate_bitcast_fusion
  85.6 6.2 convolution_bitcast_fusion
  92.3 5.8 copy.180
  98.0 4.8 all-to-all-start
  103.7 46.5 %all-to-all-done = f32[2,11,360,101]{3,0,1,2:T(2,128)} async-done(((f32[2,11,360,101]{3,0,1,2:T(2,128)}), f32[2,11,360,101]{3,0,1,2:T(2,128)}, u32[]{:S(2)}, u32[]{:S(2)}) %all-to-all-start) | async-done | bytes 3199712 | tf_op jit(solution)/shard_map/all_to_all | solution.py:186
  150.2 8.9 %copy.264 = f32[2,11,4,90,101]{3,2,4,1,0:T(4,128)} copy(f32[2,11,4,90,101]{4,0,1,3,2:T(2,128)} %bitcast.195) | data formatting | bytes 6399360 | tf_op jit(solution)/shard_map/all_to_all | solution.py:186
  159.2 4.1 fusion.487
  163.2 2.9 copy.183
  166.2 2.4 squeeze.110
  168.5 4.1 copy.182
  172.7 3.3 squeeze.109
  176.0 6.0 fusion.26
  182.0 6.0 fusion.28
  187.9 6.2 convolution_subtract_fusion.1
  194.1 6.3 add_bitcast_fusion.2
  200.6 5.7 copy.184
  206.3 6.8 %all-to-all-start.1 = ((f32[2,11,90,384]{2,0,1,3:T(2,128)}), f32[2,11,90,384]{2,0,1,3:T(2,128)}, u32[]{:S(2)}, u32[]{:S(2)}) async-start(f32[2,11,90,384]{2,0,1,3:T(2,128)} %copy.184), calls=%async_computation.1 | async-start | bytes 8650752 | tf_op jit(solution)/shard_map/all_to_all | solution.py:203
  213.8 95.0 %all-to-all-done.1 = f32[2,11,90,384]{2,0,1,3:T(2,128)} async-done(((f32[2,11,90,384]{2,0,1,3:T(2,128)}), f32[2,11,90,384]{2,0,1,3:T(2,128)}, u32[]{:S(2)}, u32[]{:S(2)}) %all-to-all-start.1) | async-done | bytes 3041312 | tf_op jit(solution)/shard_map/all_to_all | solution.py:203
  308.8 2.7 copy.185
  312.2 2.0 fusion
  314.1 2.0 fusion.2
  316.2 2.0 fusion.8
  318.2 3.1 fusion.61
  321.3 4.0 multiply_reduce_fusion
  325.3 3.1 fusion.62
  328.4 3.2 add_bitcast_fusion.1
  331.6 3.1 subtract_bitcast_fusion.1
  335.9 99.9 %all_to_all.60 = f32[2,88,90,48]{2,3,0,1:T(8,128)S(1)} all-to-all(f32[2,88,90,48]{2,3,0,1:T(8,128)S(1)} %copy.192), channel_id=1, replica_groups=mesh['gy'=8,'gx'=4] {'gy'}, dimensions={1} | all-to-all | bytes 6082560 | tf_op jit(solution)/shard_map/all_to_all | solution.py:237
  436.1 1.7 fusion.488
  437.8 1.6 copy.196
  439.4 2.3 copy.197
  441.8 3.2 copy.194
  445.0 2.5 copy.195
  447.5 6.0 fusion.22
  453.5 6.5 %fusion.24 = f32[11,90,404]{2,1,0:T(8,128)S(1)} fusion(f32[11,90,384]{2,1,0:T(8,128)S(1)} %copy.197, f32[11,90,384]{2,1,0:T(8,128)S(1)} %copy.195, f32[11,384]{1,0:T(8,128)S(1)} %get-tuple-element.979, f32[11,384]{1,0:T(8,128)S(1)} %get-tuple-element.978, s32[404]{0:T(512)S(1)} %fusion.357), kind=kOutput, calls=%fused_computation.45 | convolution fusion | flops 1845552384 | bytes 4676528 | tf_op jit(solution)/shard_map/ykm,xm->ykx/dot_general | solution.py:105
  460.0 6.0 add_bitcast_fusion
  466.1 6.0 subtract_bitcast_fusion
  472.1 2.8 pad_maximum_fusion.1
  474.9 9.1 %copy.200 = f32[2,11,90,404]{2,0,1,3:T(2,128)} copy(f32[2,11,90,404]{3,2,1,0:T(8,128)} %pad_maximum_fusion.1) | data formatting | bytes 6399360 | tf_op jit(solution)/shard_map/stack | solution.py:244
  484.0 5.1 all-to-all-start.3
  514.4 58.7 %psum.7 = f32[1]{0:T(128)} all-reduce(f32[1]{0:T(128)} %bitcast.284), channel_id=1, replica_groups=mesh['gy'=8,'gx'=4] {'gy','gx'}, use_global_device_ids=true, to_apply=%region_61.62 | all-reduce | flops 1 | bytes 8 | tf_op jit(solution)/shard_map/psum | solution.py:232
  573.1 8.9 %copy.265 = f32[2,11,90,4,101]{4,3,0,2,1:T(4,128)} copy(f32[2,11,90,4,101]{2,0,1,4,3:T(2,128)} %bitcast.216) | data formatting | bytes 6399360 | tf_op jit(solution)/shard_map/all_to_all | solution.py:243
  582.0 4.4 fusion.490
  586.5 3.5 copy.203
  590.0 2.8 squeeze.116
  592.8 3.7 copy.202
  596.5 2.8 squeeze.115
  599.2 7.5 %fusion.47 = f32[11,101,360]{2,1,0:T(8,128)S(1)} fusion(f32[11,360,101]{1,2,0:T(8,128)} %squeeze.115), kind=kOutput, calls=%fused_computation.62 | convolution fusion | flops 1728993536 | bytes 3199680 | tf_op jit(solution)/shard_map/ykx,zk->yxz/dot_general | solution.py:105
  606.8 6.2 convolution_subtract_fusion
  614.6 1.9 multiply_reduce_fusion.5
  616.5 1.2 fusion.370
  618.5 1.8 multiply_reduce_fusion.10
  621.7 1.2 multiply_reduce_fusion.15
  (858 shorter events, 84.2 us)
Async XLA Ops:
  0.6 32.9 %copy-start.71 = (f32[3,384]{1,0:T(4,128)S(1)}, f32[3,384]{1,0:T(4,128)}, u32[]{:S(2)}) copy-start(f32[3,384]{1,0:T(4,128)} %param.19) | copy-start | bytes 13828
  22.5 22.6 %copy-start.156 = (f32[64]{0:T(128)}, f32[64]{0:T(128)S(1)}, u32[]{:S(2)}) copy-start(f32[64]{0:T(128)S(1)} %fusion.371) | copy-start | bytes 772
  23.2 21.9 %copy-start.152 = (f32[64]{0:T(128)}, f32[64]{0:T(128)S(1)}, u32[]{:S(2)}) copy-start(f32[64]{0:T(128)S(1)} %fusion.375) | copy-start | bytes 772
  23.7 21.3 %copy-start.150 = (f32[64]{0:T(128)}, f32[64]{0:T(128)S(1)}, u32[]{:S(2)}) copy-start(f32[64]{0:T(128)S(1)} %fusion.377) | copy-start | bytes 772
  24.4 20.7 %copy-start.148 = (f32[64]{0:T(128)}, f32[64]{0:T(128)S(1)}, u32[]{:S(2)}) copy-start(f32[64]{0:T(128)S(1)} %fusion.379) | copy-start | bytes 772
  25.1 20.0 %copy-start.146 = (f32[64]{0:T(128)}, f32[64]{0:T(128)S(1)}, u32[]{:S(2)}) copy-start(f32[64]{0:T(128)S(1)} %fusion.381) | copy-start | bytes 772
  25.7 19.4 %copy-start.154 = (f32[64]{0:T(128)}, f32[64]{0:T(128)S(1)}, u32[]{:S(2)}) copy-start(f32[64]{0:T(128)S(1)} %fusion.373) | copy-start | bytes 772
  31.1 15.3 %copy-start.127 = (f32[64]{0:T(128)}, f32[64]{0:T(128)S(1)}, u32[]{:S(2)}) copy-start(f32[64]{0:T(128)S(1)} %get-tuple-element.988) | copy-start | bytes 772
  40.2 6.2 copy-start.2
  40.8 16.6 %copy-start.8 = (f32[3,64,360]{2,1,0:T(8,128)}, f32[3,64,360]{2,1,0:T(8,128)S(1)}, u32[]{:S(2)}) copy-start(f32[3,64,360]{2,1,0:T(8,128)S(1)} %multiply_add_fusion.3) | copy-start | bytes 829444
  41.3 9.1 %copy-start.4 = (f32[3,64,360]{2,1,0:T(8,128)}, f32[3,64,360]{2,1,0:T(8,128)S(1)}, u32[]{:S(2)}) copy-start(f32[3,64,360]{2,1,0:T(8,128)S(1)} %multiply_add_fusion.6) | copy-start | bytes 829444
  41.7 6.4 %copy-start.10 = (f32[3,64,360]{2,1,0:T(8,128)}, f32[3,64,360]{2,1,0:T(8,128)S(1)}, u32[]{:S(2)}) copy-start(f32[3,64,360]{2,1,0:T(8,128)S(1)} %multiply_add_fusion.5) | copy-start | bytes 829444
  42.4 12.7 %copy-start.6 = (f32[3,64,360]{2,1,0:T(8,128)}, f32[3,64,360]{2,1,0:T(8,128)S(1)}, u32[]{:S(2)}) copy-start(f32[3,64,360]{2,1,0:T(8,128)S(1)} %multiply_add_fusion.8) | copy-start | bytes 829444
  43.5 9.4 %copy-start.12 = (f32[3,64,360]{2,1,0:T(8,128)}, f32[3,64,360]{2,1,0:T(8,128)S(1)}, u32[]{:S(2)}) copy-start(f32[3,64,360]{2,1,0:T(8,128)S(1)} %multiply_add_fusion.7) | copy-start | bytes 829444
  70.5 9.1 %copy-start.14 = (f32[11,21,360]{2,1,0:T(8,128)S(1)}, f32[11,21,360]{2,1,0:T(8,128)}, u32[]{:S(2)}) copy-start(f32[11,21,360]{2,1,0:T(8,128)} %reshape.4064) | copy-start | bytes 997924
  98.0 52.2 %all-to-all-start = ((f32[2,11,360,101]{3,0,1,2:T(2,128)}), f32[2,11,360,101]{3,0,1,2:T(2,128)}, u32[]{:S(2)}, u32[]{:S(2)}) async-start(f32[2,11,360,101]{3,0,1,2:T(2,128)} %copy.180), calls=%async_computation | async-start | bytes 8110080 | tf_op jit(solution)/shard_map/all_to_all | solution.py:186
  176.0 6.0 copy-start
  206.3 102.5 %all-to-all-start.1 = ((f32[2,11,90,384]{2,0,1,3:T(2,128)}), f32[2,11,90,384]{2,0,1,3:T(2,128)}, u32[]{:S(2)}, u32[]{:S(2)}) async-start(f32[2,11,90,384]{2,0,1,3:T(2,128)} %copy.184), calls=%async_computation.1 | async-start | bytes 8650752 | tf_op jit(solution)/shard_map/all_to_all | solution.py:203
  484.0 5.1 copy-start.28
  484.0 5.9 copy-start.16
  484.0 6.6 %copy-start.30 = (f32[64,231]{0,1:T(8,128)S(1)}, f32[64,231]{0,1:T(8,128)}, u32[]{:S(2)}) copy-start(f32[64,231]{0,1:T(8,128)} %copy-done.29) | copy-start | bytes 177412
  484.0 7.3 %copy-start.32 = (f32[64,231]{0,1:T(8,128)S(1)}, f32[64,231]{0,1:T(8,128)}, u32[]{:S(2)}) copy-start(f32[64,231]{0,1:T(8,128)} %copy-done.31) | copy-start | bytes 177412
  484.0 8.0 %copy-start.18 = (f32[64,231]{0,1:T(8,128)S(1)}, f32[64,231]{0,1:T(8,128)}, u32[]{:S(2)}) copy-start(f32[64,231]{0,1:T(8,128)} %copy-done.17) | copy-start | bytes 177412
  484.0 8.7 %copy-start.34 = (f32[64,231]{0,1:T(8,128)S(1)}, f32[64,231]{0,1:T(8,128)}, u32[]{:S(2)}) copy-start(f32[64,231]{0,1:T(8,128)} %copy-done.33) | copy-start | bytes 177412
  484.0 9.4 %copy-start.36 = (f32[64,231]{0,1:T(8,128)S(1)}, f32[64,231]{0,1:T(8,128)}, u32[]{:S(2)}) copy-start(f32[64,231]{0,1:T(8,128)} %copy-done.35) | copy-start | bytes 177412
  484.0 10.1 %copy-start.20 = (f32[64,231]{0,1:T(8,128)S(1)}, f32[64,231]{0,1:T(8,128)}, u32[]{:S(2)}) copy-start(f32[64,231]{0,1:T(8,128)} %copy-done.19) | copy-start | bytes 177412
  484.0 10.8 %copy-start.38 = (f32[64,231]{0,1:T(8,128)S(1)}, f32[64,231]{0,1:T(8,128)}, u32[]{:S(2)}) copy-start(f32[64,231]{0,1:T(8,128)} %copy-done.37) | copy-start | bytes 177412
  484.0 89.1 %all-to-all-start.3 = ((f32[2,11,90,404]{2,0,1,3:T(2,128)}), f32[2,11,90,404]{2,0,1,3:T(2,128)}, u32[]{:S(2)}, u32[]{:S(2)}) async-start(f32[2,11,90,404]{2,0,1,3:T(2,128)} %copy.200), calls=%async_computation.3 | async-start | bytes 9101312 | tf_op jit(solution)/shard_map/all_to_all | solution.py:243
  489.1 6.4 %copy-start.40 = (f32[64,231]{0,1:T(8,128)S(1)}, f32[64,231]{0,1:T(8,128)}, u32[]{:S(2)}) copy-start(f32[64,231]{0,1:T(8,128)} %copy-done.39) | copy-start | bytes 177412
  489.1 7.1 %copy-start.22 = (f32[64,231]{0,1:T(8,128)S(1)}, f32[64,231]{0,1:T(8,128)}, u32[]{:S(2)}) copy-start(f32[64,231]{0,1:T(8,128)} %copy-done.21) | copy-start | bytes 177412
  489.1 7.8 %copy-start.42 = (f32[64,231]{0,1:T(8,128)S(1)}, f32[64,231]{0,1:T(8,128)}, u32[]{:S(2)}) copy-start(f32[64,231]{0,1:T(8,128)} %copy-done.41) | copy-start | bytes 177412
  489.1 8.5 %copy-start.44 = (f32[64,231]{0,1:T(8,128)S(1)}, f32[64,231]{0,1:T(8,128)}, u32[]{:S(2)}) copy-start(f32[64,231]{0,1:T(8,128)} %copy-done.43) | copy-start | bytes 177412
  489.1 8.6 %copy-start.24 = (f32[64,231]{0,1:T(8,128)S(1)}, f32[64,231]{0,1:T(8,128)}, u32[]{:S(2)}) copy-start(f32[64,231]{0,1:T(8,128)} %copy-done.23) | copy-start | bytes 177412
  489.2 8.7 %copy-start.46 = (f32[64,231]{0,1:T(8,128)S(1)}, f32[64,231]{0,1:T(8,128)}, u32[]{:S(2)}) copy-start(f32[64,231]{0,1:T(8,128)} %copy-done.45) | copy-start | bytes 177412
  489.2 9.4 %copy-start.48 = (f32[64,231]{0,1:T(8,128)S(1)}, f32[64,231]{0,1:T(8,128)}, u32[]{:S(2)}) copy-start(f32[64,231]{0,1:T(8,128)} %copy-done.47) | copy-start | bytes 177412
  489.2 10.1 %copy-start.26 = (f32[64,231]{0,1:T(8,128)S(1)}, f32[64,231]{0,1:T(8,128)}, u32[]{:S(2)}) copy-start(f32[64,231]{0,1:T(8,128)} %copy-done.25) | copy-start | bytes 177412
  489.2 10.8 %copy-start.50 = (f32[64,231]{0,1:T(8,128)S(1)}, f32[64,231]{0,1:T(8,128)}, u32[]{:S(2)}) copy-start(f32[64,231]{0,1:T(8,128)} %copy-done.49) | copy-start | bytes 177412
  489.2 11.5 %copy-start.53 = (f32[64,11,21]{0,2,1:T(8,128)S(1)}, f32[64,11,21]{0,2,1:T(8,128)}, u32[]{:S(2)}) copy-start(f32[64,11,21]{0,2,1:T(8,128)} %get-tuple-element.475) | copy-start | bytes 177412
  491.3 10.1 %copy-start.52 = (f32[64,11,21]{0,2,1:T(8,128)S(1)}, f32[64,11,21]{0,2,1:T(8,128)}, u32[]{:S(2)}) copy-start(f32[64,11,21]{0,2,1:T(8,128)} %get-tuple-element.625) | copy-start | bytes 177412
  492.7 9.4 %copy-start.51 = (f32[64,11,21]{0,2,1:T(8,128)S(1)}, f32[64,11,21]{0,2,1:T(8,128)}, u32[]{:S(2)}) copy-start(f32[64,11,21]{0,2,1:T(8,128)} %get-tuple-element.627) | copy-start | bytes 177412
  494.8 8.0 %copy-start.56 = (f32[64,11,21]{0,2,1:T(8,128)S(1)}, f32[64,11,21]{0,2,1:T(8,128)}, u32[]{:S(2)}) copy-start(f32[64,11,21]{0,2,1:T(8,128)} %get-tuple-element.480) | copy-start | bytes 177412
  496.3 7.3 %copy-start.55 = (f32[64,11,21]{0,2,1:T(8,128)S(1)}, f32[64,11,21]{0,2,1:T(8,128)}, u32[]{:S(2)}) copy-start(f32[64,11,21]{0,2,1:T(8,128)} %get-tuple-element.621) | copy-start | bytes 177412
  497.7 6.7 %copy-start.54 = (f32[64,11,21]{0,2,1:T(8,128)S(1)}, f32[64,11,21]{0,2,1:T(8,128)}, u32[]{:S(2)}) copy-start(f32[64,11,21]{0,2,1:T(8,128)} %get-tuple-element.623) | copy-start | bytes 177412
  498.6 6.5 %copy-start.59 = (f32[64,11,21]{0,2,1:T(8,128)S(1)}, f32[64,11,21]{0,2,1:T(8,128)}, u32[]{:S(2)}) copy-start(f32[64,11,21]{0,2,1:T(8,128)} %get-tuple-element.485) | copy-start | bytes 177412
  500.0 5.8 copy-start.58
  500.7 5.8 copy-start.57
  501.4 5.8 copy-start.62
  502.1 5.8 copy-start.61
  502.9 5.8 copy-start.60
  503.6 5.8 copy-start.65
  504.3 5.8 copy-start.64
  505.1 5.8 copy-start.63
  505.8 5.8 copy-start.68
  506.5 5.8 copy-start.67
  507.2 5.8 copy-start.66
  599.2 7.5 %copy-start.1 = (f32[11,360,101]{1,2,0:T(8,128)S(1)}, f32[11,360,101]{1,2,0:T(8,128)}, u32[]{:S(2)}) copy-start(f32[11,360,101]{1,2,0:T(8,128)} %squeeze.116) | copy-start | bytes 4799524
  613.2 4.6 copy-start.3
  614.6 3.9 copy-start.87
  614.6 3.9 copy-start.88
  614.6 3.9 copy-start.89
  616.5 4.5 copy-start.11
  617.8 3.9 copy-start.79
  617.8 3.9 copy-start.80
  617.8 3.9 copy-start.81
  (98 other events, 224.8 us)
where the time goes:
time: 644 us; the launch traced here: 632 us
  blocking collectives  159 us (25%)
  local copies, waits for them, and re-layouts  148 us (23%)
  waiting for transfers between devices  142 us (22%)
  matrix products  104 us (16%)
  other arithmetic  55.8 us (9%)
  starting transfers between devices  16.7 us (3%)
  between operations  7.14 us (1%)
    dot_general x32, matrix products, contract(): return jnp.einsum(pattern, operand, matrix, precision=lax.Precision.HIGHEST)  104 us
    all_to_all x1, blocking collectives, on_device(): lax.all_to_all(jnp.stack([back_real, back_imag]), 'gy', split_axis=1, con...  99.9 us
    all_to_all x1, waiting for transfers between devices, on_device(): lax.all_to_all(twisted, 'gy', split_axis=3, concat_axis=1, tiled=True)  95 us
    psum x1, blocking collectives, on_device(): energy = lax.psum(local_energy, ('gy', 'gx'))  58.7 us
    all_to_all x1, waiting for transfers between devices, on_device(): lax.all_to_all(jnp.stack([real_part, imag_part]), 'gx', split_axis=2, con...  46.5 us
    mul x84, local copies, waits for them, and re-layouts, on_device(): dense_y[r][:, :, None] * dense_x[p][:, None, :]  28.1 us
    scatter-add x5, local copies, waits for them, and re-layouts, on_device(): spread_grid = spread_grid.at[:, b * BX:b * BX + block_x, :].add(block_grid)  19.1 us
    mul x25, other arithmetic, spline_tables(): inverse_n * ((fraction + j) * current[n - 2 - j] + (n - j - fraction) * c...  13.8 us
  transfers between devices with their start and end apart: 3, of which 2 were waited for; matrix products, arithmetic and copies ran while one was open for 4% of the time, Pallas kernels for 0%

commit v1 on v0

v1 whole, which is shorter than its diff:
```python
import functools
import math

import jax
import jax.numpy as jnp
import ml_dtypes
import numpy as np
from jax import lax
from jax.experimental import pallas as pl
from jax.experimental.pallas import tpu as pltpu
from jax.sharding import PartitionSpec as P

NX = 384
NZ = 360
CY = 6
LANES = 128
UNIT_X = 32
WIN = 40
EXT = NX + 8
SCREENING = 0.9
MESH = pl.DeviceIdType.MESH
F32 = jnp.float32
BF16 = jnp.bfloat16
VMEM_LIMIT = 52 * 1024 * 1024


def spline_tables(fraction):
    levels = {2: [1.0 - fraction, fraction]}
    current = levels[2]
    for n in range(3, 7):
        inverse_n = 1.0 / (n - 1)
        updated = [None] * n
        updated[n - 1] = inverse_n * fraction * current[n - 2]
        for j in range(1, n - 1):
            updated[n - 1 - j] = inverse_n * (
                (fraction + j) * current[n - 2 - j] + (n - j - fraction) * current[n - 1 - j]
            )
        updated[0] = inverse_n * (1.0 - fraction) * current[0]
        current = updated
        levels[n] = current
    zero_row = jnp.zeros_like(fraction)

    def entry_at(values_list, k):
        return values_list[k] if 0 <= k < len(values_list) else zero_row

    first = [entry_at(levels[5], t - 1) - entry_at(levels[5], t) for t in range(6)]
    second = [
        entry_at(levels[4], t - 2) - 2.0 * entry_at(levels[4], t - 1) + entry_at(levels[4], t)
        for t in range(6)
    ]
    return [levels[6], first, second]


def split_np(table):
    high = table.astype(np.float32).astype(ml_dtypes.bfloat16)
    low = (table - high.astype(np.float64)).astype(np.float32).astype(ml_dtypes.bfloat16)
    return high, low


def split(x):
    high = x.astype(BF16)
    return high, (x - high.astype(F32)).astype(BF16)


NN = (((1,), (0,)), ((), ()))
NT = (((1,), (1,)), ((), ()))
CHUNKS = ((0, 256), (256, 128))


def dot(left, right, dims):
    return lax.dot_general(left, right, dims, preferred_element_type=F32)


def dot3(left, right_high, right_low, dims):
    m = left.shape[0] // 2
    both = dot(left, right_high, dims)
    return both[:m] + (both[m:] + dot(left[:m], right_low, dims))


def stacked(x):
    return jnp.concatenate(split(x), axis=0)


def x_tables():
    ticks = np.outer(np.arange(NX), np.arange(NX)) % NX
    angles = 2.0 * np.pi / NX * ticks
    return np.concatenate([np.cos(angles), -np.sin(angles)], axis=0)


def y_tables(groups, kzp, rows_pad):
    ny = CY * groups
    ticks = np.outer(np.arange(ny), np.arange(ny)) % ny
    angles = 2.0 * np.pi / ny * ticks
    cos, sin = np.cos(angles), np.sin(angles)
    table = np.zeros((2, kzp, ny, groups, rows_pad))
    for k in range(kzp):
        for y in range(CY):
            at_y = np.arange(groups) * CY + y
            for c in range(2):
                row = (c * CY + y) * kzp + k
                if c == 0:
                    table[0, k, :, :, row] = cos[:, at_y]
                    table[1, k, :, :, row] = -sin[:, at_y]
                else:
                    table[0, k, :, :, row] = sin[:, at_y]
                    table[1, k, :, :, row] = cos[:, at_y]
    return table.reshape(2 * ny * kzp, groups * rows_pad)


def my_group(groups, pencils):
    flat = lax.axis_index("gy") * pencils + lax.axis_index("gx")
    return flat // groups, lax.rem(flat, groups)


def place(groups, pencils, g, s):
    flat = g * groups + s
    return flat // pencils, lax.rem(flat, pencils)


def ring_targets(groups, pencils, g, s):
    flat = g * groups + s
    home, pencil = flat // pencils, lax.rem(flat, pencils)
    found = []
    for v in range(2):
        for other in range(pencils):
            found.append((other, lax.rem(home + v, groups), v * pencils + pencil))
    return found


def ring_sources(groups, pencils, g, s):
    found = []
    for v in range(2):
        for j in range(pencils):
            flat = lax.rem(s - v + groups, groups) * pencils + j
            found.append((flat // groups, lax.rem(flat, groups), v * pencils + j))
    return found


def turn(ticks, period):
    quarter = jnp.floor(ticks * (4.0 / period) + 0.5)
    x = (ticks - (period / 4.0) * quarter) * (2.0 * math.pi / period)
    quarter = quarter - 4.0 * jnp.floor(quarter * 0.25)
    x2 = x * x
    sin = x + x * x2 * (
        -1.0 / 6.0 + x2 * (1.0 / 120.0 + x2 * (-1.0 / 5040.0 + x2 * (1.0 / 362880.0)))
    )
    cos = 1.0 + x2 * (
        -0.5 + x2 * (1.0 / 24.0 + x2 * (-1.0 / 720.0 + x2 * (1.0 / 40320.0)))
    )
    odd = (quarter == 1.0) | (quarter == 3.0)
    first, second = jnp.where(odd, sin, cos), jnp.where(odd, cos, sin)
    first = jnp.where((quarter == 1.0) | (quarter == 2.0), -first, first)
    second = jnp.where(quarter >= 2.0, -second, second)
    return first, second


def modulus(cos):
    return (64.0 + 52.0 * cos + 4.0 * cos * cos) * (1.0 / 120.0)


def dense_rows(tables, row, base, rows):
    index = lax.broadcasted_iota(jnp.int32, (rows, LANES), 0).astype(F32) - base
    at = [index == float(t) for t in range(6)]
    found = []
    for order in range(3):
        total = jnp.zeros((rows, LANES), F32)
        for t in range(6):
            total = jnp.where(at[t], tables[order][t][row : row + 1], total)
        found.append(total)
    return found


def mode_weights(tables, cell_z, kz, step_ref):
    cell_cos, cell_sin = turn(kz * cell_z, float(NZ))
    found = []
    for order in range(3):
        fc, fs = 0.0, 0.0
        for t in range(6):
            weight = tables[order][t][2:3]
            fc = fc + weight * step_ref[2 * t]
            fs = fs + weight * step_ref[2 * t + 1]
        found.append(
            jnp.concatenate(
                [cell_cos * fc - cell_sin * fs, cell_sin * fc + cell_cos * fs], axis=0
            )
        )
    return found


def fill_phases(phase_ref, s, groups, shear):
    ny = CY * groups
    shape = (2 * CY, NX)
    row = lax.broadcasted_iota(jnp.int32, shape, 0)
    col = lax.broadcasted_iota(jnp.int32, shape, 1)
    kx = jnp.where(col < NX // 2, col, col - NX)
    wrap = jnp.where(s == 0, ny, 0)
    y = s * CY + jnp.where(row < CY, row, row - CY + wrap)
    ticks = y * shear * kx
    period = NX * ny
    count = jnp.floor(ticks.astype(F32) * (1.0 / period)).astype(jnp.int32)
    cos, sin = turn((ticks - count * period).astype(F32), float(period))
    phase_ref[0] = cos
    phase_ref[1] = sin


def fill_green(gtab_ref, g, s, groups, kz_part, kzp, shear):
    ny = CY * groups
    shape = (ny, NX)
    row = lax.broadcasted_iota(jnp.int32, shape, 0)
    col = lax.broadcasted_iota(jnp.int32, shape, 1)
    kx = jnp.where(col < NX // 2, col, col - NX)
    ky = jnp.where(row < ny // 2, row, row - ny)
    fx, fy = kx.astype(F32), ky.astype(F32)
    wave = fy + fx * shear.astype(F32) * (1.0 / NX)
    plane = (fx * (1.0 / NX)) * (fx * (1.0 / NX)) + (wave * (1.0 / ny)) * (wave * (1.0 / ny))
    rate = -((math.pi / SCREENING) ** 2)
    cos_w, _ = turn((ky * NX + kx * shear).astype(F32), float(NX * ny))
    cos_x, _ = turn(fx, float(NX))
    mod_xy = modulus(cos_w) * modulus(cos_x)
    edge = (kx == -(NX // 2)) | (ky == -(ny // 2))
    front = jnp.where(edge, 0.0, jnp.exp(rate * plane) / (math.pi * mod_xy * mod_xy))
    origin = (kx == 0) & (ky == 0)
    for i in range(kzp):
        local = s * kzp + i
        kz = g * kz_part + local
        fz = jnp.full((1, NX), kz.astype(F32), F32)
        part_z = (fz * (1.0 / NZ)) * (fz * (1.0 / NZ))
        cos_z, _ = turn(fz, float(NZ))
        mod_z = modulus(cos_z)
        weight = jnp.where(fz == 0.0, 1.0, 2.0) * (1.0 / (NX * ny * NZ))
        used = (local < kz_part) & (kz < NZ // 2)
        front_z = jnp.where(used, weight * jnp.exp(rate * part_z) / (mod_z * mod_z), 0.0)
        zero = origin & (fz == 0.0)
        norm = jnp.where(zero, 1.0, plane + part_z)
        gtab_ref[i * ny : (i + 1) * ny] = jnp.where(zero, 0.0, front * front_z / norm)


def whole_kernel(
    groups, pencils, per_pencil, blocks, kz_part, kzt, kzp, rows_pad,
    cell_ref, off_ref, charge_ref, dip_ref, count_ref, shear_ref,
    cf_high_hbm, cf_low_hbm, c_hbm, w1_hbm, w2_hbm,
    out_ref,
    cf_high, cf_low, c_both, w1_both, w2_both,
    own, gathered, weights, z_high, z_low, cells, lhs, rhs_high, rhs_low,
    send, arrived, filtered, back, gtab_ref, phase_ref, step_ref, shares, parts, held,
    const_sem, get_send, get_recv, out_send, out_recv, back_send, back_recv,
    told_send, told_recv, ret_send, ret_recv,
):
    g, s = my_group(groups, pencils)
    ny = CY * groups
    zr = 2 * kzt
    modes = ny * kzp
    shear = shear_ref[0]
    targets = ring_targets(groups, pencils, g, s)
    sources = ring_sources(groups, pencils, g, s)
    peers = [lax.rem(s + k, groups) for k in range(1, groups)]

    barrier = pltpu.get_barrier_semaphore()
    for pg, ps, _ in sources + targets:
        pl.semaphore_signal(
            barrier, inc=1, device_id=place(groups, pencils, pg, ps), device_id_type=MESH
        )
    for p in peers:
        pl.semaphore_signal(
            barrier, inc=1, device_id=place(groups, pencils, g, p), device_id_type=MESH
        )

    loads = [
        pltpu.make_async_copy(source, target, const_sem.at[i])
        for i, (source, target) in enumerate(
            [
                (cf_high_hbm, cf_high),
                (cf_low_hbm, cf_low),
                (w1_hbm, w1_both),
                (w2_hbm, w2_both),
                (c_hbm, c_both),
            ]
        )
    ]
    for load in loads:
        load.start()

    atoms = own.shape[1]
    per_block = atoms // blocks
    lane = lax.broadcasted_iota(jnp.int32, (1, atoms), 1)
    live = jnp.zeros((1, atoms), F32)
    for b in range(blocks):
        first = b * per_block
        live = jnp.where((lane >= first) & (lane < first + count_ref[b]), 1.0, live)
    own[...] = jnp.concatenate(
        [
            cell_ref[...].astype(F32),
            off_ref[...],
            charge_ref[...] * live,
            dip_ref[...] * live,
            jnp.zeros((6, atoms), F32),
        ],
        axis=0,
    )
    pl.semaphore_wait(barrier, len(sources) + len(targets) + len(peers))

    def get_copy(i, pg, ps, slot):
        return pltpu.make_async_remote_copy(
            src_ref=own,
            dst_ref=gathered.at[slot],
            send_sem=get_send.at[i],
            recv_sem=get_recv.at[slot],
            device_id=place(groups, pencils, pg, ps),
            device_id_type=MESH,
        )

    for i, (pg, ps, slot) in enumerate(targets):
        here = (pg == g) & (ps == s)

        @pl.when(jnp.logical_not(here))
        def _():
            get_copy(i, pg, ps, slot).start()

        @pl.when(here)
        def _():
            gathered[slot] = own[...]

    fill_phases(phase_ref, s, groups, shear)
    fill_green(gtab_ref, g, s, groups, kz_part, kzp, shear)
    kz = (lax.broadcasted_iota(jnp.int32, (kzt, LANES), 0) + g * kz_part).astype(F32)
    for t in range(6):
        cos, sin = turn(kz * float(t), float(NZ))
        step_ref[2 * t] = cos
        step_ref[2 * t + 1] = sin
    cells[...] = jnp.zeros_like(cells)
    used = 2 * CY * kzp
    if rows_pad > used:
        for p in range(groups):
            send[p, used:rows_pad] = jnp.zeros((rows_pad - used, NX), F32)

    for pg, ps, slot in sources:
        here = (pg == g) & (ps == s)

        @pl.when(jnp.logical_not(here))
        def _():
            get_copy(0, pg, ps, slot).wait_recv()

    slab_low = lax.rem(s - 1 + groups, groups)
    y_base = [(s * CY).astype(F32), (slab_low * CY + CY).astype(F32)]

    def spread(j, carry):
        for k in range(per_pencil):
            x_at = pl.multiple_of((j * per_pencil + k) * UNIT_X, UNIT_X)
            x_base = x_at.astype(F32)
            for v in range(2):
                unit = (j * 2 + v) * per_pencil + k
                atom = gathered[v * pencils + j, :, k * LANES : (k + 1) * LANES]
                tables = spline_tables(atom[3:6])
                wx = dense_rows(tables, 0, atom[0:1] - x_base, WIN)
                wy = dense_rows(tables, 1, atom[1:2] - y_base[v], 8)
                z0, z1, z2 = mode_weights(tables, atom[2:3], kz, step_ref)
                weights[unit] = jnp.concatenate(wx + wy, axis=0)
                high, low = split(jnp.concatenate([z0, z1, z2], axis=1))
                z_high[unit] = high
                z_low[unit] = low
                q, mx, my, mz = (atom[i : i + 1] for i in range(6, 10))
                right = jnp.concatenate([q * z0 + mz * z1, z0], axis=1)
                mux_x = mx * wx[1]
                muy_x = my * wx[0]
                left = jnp.concatenate(
                    [
                        jnp.concatenate(
                            [
                                wy[0][y : y + 1] * wx[0],
                                wy[0][y : y + 1] * mux_x + wy[1][y : y + 1] * muy_x,
                            ],
                            axis=1,
                        )
                        for y in range(CY)
                    ],
                    axis=0,
                )
                part = dot3(stacked(left), *split(right), NT)
                for y in range(CY):
                    here = cells.at[v * CY + y, pl.ds(x_at, WIN), pl.ds(0, zr)]
                    here[...] = here[...] + part[y * WIN : (y + 1) * WIN]
        return carry

    lax.fori_loop(0, pencils, spread, 0)

    total = 2 * CY * zr
    for at in range(2 * CY):
        cells[at, 0:8] = cells[at, 0:8] + cells[at, NX:EXT]
        turned = jnp.transpose(cells[at, 0:NX])
        cos_part, sin_part = turned[0:kzt], turned[kzt:zr]
        high, low = split(
            jnp.concatenate(
                [
                    jnp.concatenate([cos_part, sin_part], axis=1),
                    jnp.concatenate([-sin_part, cos_part], axis=1),
                ],
                axis=0,
            )
        )
        lhs[at * zr : (at + 1) * zr] = high
        lhs[total + at * zr : total + (at + 1) * zr] = low

    def chunk_copies(source, target, send_sems, recv_sems, chunk):
        first, count = CHUNKS[chunk]
        return [
            pltpu.make_async_remote_copy(
                src_ref=source.at[p, :, pl.ds(first, count)],
                dst_ref=target.at[s, :, pl.ds(first, count)],
                send_sem=send_sems.at[chunk, k],
                recv_sem=recv_sems.at[chunk, k],
                device_id=place(groups, pencils, g, p),
                device_id_type=MESH,
            )
            for k, p in enumerate(peers)
        ]

    loads[0].wait()
    loads[1].wait()
    sent = []
    for chunk, (first, count) in enumerate(CHUNKS):
        cols = slice(first, first + count)
        lines = dot3(lhs[...], cf_high[:, cols], cf_low[:, cols], NN)
        for y in range(CY):
            real, imag = 0.0, 0.0
            for v in range(2):
                at = v * CY + y
                ct, st = phase_ref[0, at : at + 1, cols], phase_ref[1, at : at + 1, cols]
                re = lines[at * zr : at * zr + kzt]
                im = lines[at * zr + kzt : (at + 1) * zr]
                real = real + (re * ct + im * st)
                imag = imag + (im * ct - re * st)
            for c, values in enumerate((real, imag)):
                row = (c * CY + y) * kzp
                for p in range(groups):
                    send[p, row : row + kzp, cols] = values[p * kzp : (p + 1) * kzp]
        copies = chunk_copies(send, arrived, out_send, out_recv, chunk)
        for copy in copies:
            copy.start()
        arrived[s, :, cols] = send[s, :, cols]
        sent.append(copies)

    loads[2].wait()
    loads[3].wait()
    returned = []
    power = jnp.zeros((8, LANES), F32)
    flat = groups * rows_pad
    for chunk, (first, count) in enumerate(CHUNKS):
        cols = slice(first, first + count)
        for copy in sent[chunk]:
            copy.wait_recv()
        high, low = split(arrived[:, :, cols].reshape(flat, count))
        spectrum = dot3(w1_both[...], high, low, NN)
        real, imag = spectrum[:modes], spectrum[modes:]
        gtab = gtab_ref[:, cols]
        amount = jnp.sum(
            (gtab * (real * real + imag * imag)).reshape(modes // 8, 8, count), axis=0
        )
        for i in range(0, count, LANES):
            power = power + amount[:, i : i + LANES]
        high, low = split(jnp.concatenate([gtab * real, gtab * imag], axis=0))
        filtered[:, :, cols] = dot3(w2_both[...], high, low, NN).reshape(groups, rows_pad, count)
        copies = chunk_copies(filtered, back, back_send, back_recv, chunk)
        for copy in copies:
            copy.start()
        back[s, :, cols] = filtered[s, :, cols]
        returned.append(copies)
    shares[s] = power
    told = [
        pltpu.make_async_remote_copy(
            src_ref=shares.at[s],
            dst_ref=shares.at[s],
            send_sem=told_send.at[k],
            recv_sem=told_recv.at[k],
            device_id=place(groups, pencils, g, p),
            device_id_type=MESH,
        )
        for k, p in enumerate(peers)
    ]
    for copy in told:
        copy.start()

    loads[4].wait()
    for chunk, (first, count) in enumerate(CHUNKS):
        cols = slice(first, first + count)
        deep = slice(2 * first, 2 * (first + count))
        for copy in returned[chunk]:
            copy.wait_recv()
        for y in range(CY):
            found = []
            for c in range(2):
                row = (c * CY + y) * kzp
                found.append(
                    jnp.concatenate(
                        [back[p, row : row + kzp, cols] for p in range(groups)], axis=0
                    )
                )
            real, imag = found
            for v in range(2):
                at = v * CY + y
                ct, st = phase_ref[0, at : at + 1, cols], phase_ref[1, at : at + 1, cols]
                pr = real * ct - imag * st
                pi = imag * ct + real * st
                rows = [
                    jnp.concatenate([pr, pi], axis=1),
                    jnp.concatenate([-pi, pr], axis=1),
                ]
                if zr < LANES:
                    rows.append(jnp.zeros((LANES - zr, 2 * count), F32))
                high, low = split(jnp.concatenate(rows, axis=0))
                rhs_high[at * LANES : (at + 1) * LANES, deep] = high
                rhs_low[at * LANES : (at + 1) * LANES, deep] = low
        for pair in range(CY):
            at = pair * 2 * LANES
            found = dot3(
                c_both[:, deep],
                rhs_high[at : at + 2 * LANES, deep],
                rhs_low[at : at + 2 * LANES, deep],
                NT,
            )
            for half in range(2):
                here = cells.at[2 * pair + half, 0:NX]
                part = found[:, half * LANES : (half + 1) * LANES]
                here[...] = part if chunk == 0 else here[...] + part
    for at in range(2 * CY):
        cells[at, NX:EXT] = cells[at, 0:8]

    for copy in told:
        copy.wait_recv()
    share = jnp.sum(jnp.sum(shares[...], axis=0), axis=0, keepdims=True)
    share = jnp.broadcast_to(0.25 * jnp.sum(share, axis=1, keepdims=True), (1, LANES))

    def return_copy(slot, to_slot, pg, ps):
        return pltpu.make_async_remote_copy(
            src_ref=parts.at[slot],
            dst_ref=held.at[to_slot],
            send_sem=ret_send.at[slot],
            recv_sem=ret_recv.at[to_slot],
            device_id=place(groups, pencils, pg, ps),
            device_id_type=MESH,
        )

    def sample(j, carry):
        for k in range(per_pencil):
            x_at = pl.multiple_of((j * per_pencil + k) * UNIT_X, UNIT_X)
            for v in range(2):
                unit = (j * 2 + v) * per_pencil + k
                slot = v * pencils + j
                left = jnp.concatenate(
                    [cells[v * CY + y, pl.ds(x_at, WIN), pl.ds(0, zr)] for y in range(CY)],
                    axis=0,
                )
                proj = dot3(stacked(left), z_high[unit], z_low[unit], NN)
                wx = [weights[unit, o * WIN : (o + 1) * WIN] for o in range(3)]
                wy = [weights[unit, 3 * WIN + o * 8 : 3 * WIN + (o + 1) * 8] for o in range(3)]

                def over_y(r, order):
                    return sum(
                        wy[r][y : y + 1]
                        * proj[y * WIN : (y + 1) * WIN, order * LANES : (order + 1) * LANES]
                        for y in range(CY)
                    )

                def over_x(p, values):
                    return jnp.sum(wx[p] * values, axis=0, keepdims=True)

                q00, q10, q01 = over_y(0, 0), over_y(1, 0), over_y(0, 1)
                s000, s100, s200 = over_x(0, q00), over_x(1, q00), over_x(2, q00)
                s010, s110 = over_x(0, q10), over_x(1, q10)
                s001, s101 = over_x(0, q01), over_x(1, q01)
                s020 = over_x(0, over_y(2, 0))
                s002 = over_x(0, over_y(0, 2))
                s011 = over_x(0, over_y(1, 1))
                atom = gathered[slot, :, k * LANES : (k + 1) * LANES]
                q, mx, my, mz = (atom[i : i + 1] for i in range(6, 10))
                parts[slot, :, k * LANES : (k + 1) * LANES] = jnp.concatenate(
                    [
                        s000,
                        s100,
                        s010,
                        s001,
                        q * s100 + mx * s200 + my * s110 + mz * s101,
                        q * s010 + mx * s110 + my * s020 + mz * s011,
                        q * s001 + mx * s101 + my * s011 + mz * s002,
                        share,
                    ],
                    axis=0,
                )
        return carry

    lax.fori_loop(0, pencils, sample, 0)

    for i, (pg, ps, _) in enumerate(sources):
        here = (pg == g) & (ps == s)
        to_slot = (i // pencils) * pencils + g

        @pl.when(jnp.logical_not(here))
        def _():
            return_copy(i, to_slot, pg, ps).start()

        @pl.when(here)
        def _():
            held[to_slot] = parts[i]

    for i, (pg, ps, _) in enumerate(targets):
        here = (pg == g) & (ps == s)

        @pl.when(jnp.logical_not(here))
        def _():
            return_copy(0, i, pg, ps).wait_recv()

    summed = held[0]
    for i in range(1, 2 * pencils):
        summed = summed + held[i]
    row = lax.broadcasted_iota(jnp.int32, summed.shape, 0)
    out_ref[...] = jnp.where(row < 7, summed * live, summed)

    for copies in sent + returned + [told]:
        for copy in copies:
            copy.wait_send()
    for i, (pg, ps, slot) in enumerate(targets):
        here = (pg == g) & (ps == s)

        @pl.when(jnp.logical_not(here))
        def _():
            get_copy(i, pg, ps, slot).wait_send()

    for i, (pg, ps, _) in enumerate(sources):
        here = (pg == g) & (ps == s)

        @pl.when(jnp.logical_not(here))
        def _():
            return_copy(i, 0, pg, ps).wait_send()


def on_device(groups, pencils, cell_index, offsets, charges, dipoles, block_count, shear_cells):
    atoms = charges.shape[0]
    blocks = block_count.shape[0]
    per_pencil = atoms // LANES
    units = per_pencil * pencils
    ny = CY * groups
    kz_part = -(-(NZ // 2) // pencils)
    kzp = -(-kz_part // groups)
    kzt = kzp * groups
    zr = 2 * kzt
    rows_pad = -(-2 * CY * kzp // 8) * 8
    slots = 2 * pencils

    forward = x_tables()
    backward = np.concatenate(
        [forward[half : half + NX].T[:, a : a + n] for a, n in CHUNKS for half in (0, NX)], axis=1
    )
    y_table = y_tables(groups, kzp, rows_pad)
    cf_high, cf_low = split_np(forward)
    constants = [cf_high, cf_low] + [
        np.concatenate(split_np(table), axis=0)
        for table in (backward, y_table, np.ascontiguousarray(y_table.T))
    ]
    vmem = pl.BlockSpec(memory_space=pltpu.VMEM)
    smem = pl.BlockSpec(memory_space=pltpu.SMEM)
    block = (groups, rows_pad, NX)
    peers = (groups - 1,)
    sem = pltpu.SemaphoreType.DMA
    result = pl.pallas_call(
        functools.partial(
            whole_kernel, groups, pencils, per_pencil, blocks, kz_part, kzt, kzp, rows_pad
        ),
        out_shape=jax.ShapeDtypeStruct((8, atoms), F32),
        in_specs=[vmem] * 4 + [smem] * 2 + [pl.BlockSpec(memory_space=pl.ANY)] * 5,
        out_specs=vmem,
        scratch_shapes=[
            pltpu.VMEM((2 * NX, NX), BF16),
            pltpu.VMEM((2 * NX, NX), BF16),
            pltpu.VMEM((2 * NX, 2 * NX), BF16),
            pltpu.VMEM((4 * ny * kzp, groups * rows_pad), BF16),
            pltpu.VMEM((2 * groups * rows_pad, 2 * ny * kzp), BF16),
            pltpu.VMEM((16, atoms), F32),
            pltpu.VMEM((slots, 16, atoms), F32),
            pltpu.VMEM((2 * units, 3 * WIN + 24, LANES), F32),
            pltpu.VMEM((2 * units, zr, 3 * LANES), BF16),
            pltpu.VMEM((2 * units, zr, 3 * LANES), BF16),
            pltpu.VMEM((2 * CY, EXT, LANES), F32),
            pltpu.VMEM((4 * CY * zr, 2 * NX), BF16),
            pltpu.VMEM((2 * CY * LANES, 2 * NX), BF16),
            pltpu.VMEM((2 * CY * LANES, 2 * NX), BF16),
            pltpu.VMEM(block, F32),
            pltpu.VMEM(block, F32),
            pltpu.VMEM(block, F32),
            pltpu.VMEM(block, F32),
            pltpu.VMEM((ny * kzp, NX), F32),
            pltpu.VMEM((2, 2 * CY, NX), F32),
            pltpu.VMEM((12, kzt, LANES), F32),
            pltpu.VMEM((groups, 8, LANES), F32),
            pltpu.VMEM((slots, 8, atoms), F32),
            pltpu.VMEM((slots, 8, atoms), F32),
            sem((5,)),
            sem((slots,)),
            sem((slots,)),
            sem((2,) + peers),
            sem((2,) + peers),
            sem((2,) + peers),
            sem((2,) + peers),
            sem(peers),
            sem(peers),
            sem((slots,)),
            sem((slots,)),
        ],
        compiler_params=pltpu.CompilerParams(
            collective_id=0, has_side_effects=True, vmem_limit_bytes=VMEM_LIMIT
        ),
        name="ewald",
    )(
        cell_index,
        offsets,
        charges.reshape(1, atoms),
        dipoles,
        block_count,
        shear_cells,
        *[
            jnp.asarray(t)
            for t in (constants[0], constants[1], constants[2], constants[3], constants[4])
        ],
    )
    return result[0], result[1:4], result[4:7], result[7, 0:1]


def solution(mesh):
    groups, pencils = mesh.shape["gy"], mesh.shape["gx"]
    split_all = ("gy", "gx")
    return jax.shard_map(
        functools.partial(on_device, groups, pencils),
        mesh=mesh,
        in_specs=(
            P(None, split_all),
            P(None, split_all),
            P(split_all),
            P(None, split_all),
            P(split_all),
            P(),
        ),
        out_specs=(P(split_all), P(None, split_all), P(None, split_all), P()),
        check_vma=False,
    )
```

time: 644 us -> 67.7 us (0.11)
  the two profiles are of different devices: /device:TPU:0 before, /device:TPU:5 now
where the time goes in v1:
time: 67.7 us; the launch traced here: 66.4 us
  Pallas kernels  57.8 us (85%)
  local copies, waits for them, and re-layouts  7.25 us (11%)
  between operations  1.3 us (2%)
    pallas_call x1, Pallas kernels, on_device(): pl.pallas_call(functools.partial(whole_kernel, groups, pencils, per_penci...  57.8 us
    unnamed x12, local copies, waits for them, and re-layouts  4.85 us
    slice x3, local copies, waits for them, and re-layouts, on_device(): return (result[0], result[1:4], result[4:7], result[7, 0:1])  1.71 us

profile of v1, /device:TPU:5, one launch (start us, length us, event | category | flops | bytes accessed | tf_op | source)
XLA Modules:
  0.0 66.4 jit_solution(16329704814164077446)
XLA Ops:
  0.6 0.7 %reshape.11.charge_ref = f32[1,384]{1,0:T(1,128)S(1)} reshape(f32[384]{0:T(512)} %param.13) | data formatting | bytes 3072 | tf_op jit(solution)/shard_map/reshape | solution.py:714
  2.0 0.0 copy-start
  2.0 1.1 %copy-done = bf16[768,384]{1,0:T(8,128)(2,1)S(1)} copy-done((bf16[768,384]{1,0:T(8,128)(2,1)S(1)}, bf16[768,384]{1,0:T(8,128)(2,1)}, u32[]{:S(2)}) %copy-start) | copy-done | bytes 589848
  3.0 0.0 copy-start.1
  3.0 1.1 %copy-done.1 = bf16[768,384]{1,0:T(8,128)(2,1)S(1)} copy-done((bf16[768,384]{1,0:T(8,128)(2,1)S(1)}, bf16[768,384]{1,0:T(8,128)(2,1)}, u32[]{:S(2)}) %copy-start.1) | copy-done | bytes 589848
  4.1 0.0 copy-start.2
  4.1 0.7 %copy-done.2 = s32[3,384]{1,0:T(4,128)S(1)} copy-done((s32[3,384]{1,0:T(4,128)S(1)}, s32[3,384]{1,0:T(4,128)}, u32[]{:S(2)}) %copy-start.2) | copy-done | bytes 4632
  4.8 0.0 copy-start.3
  4.8 0.7 %copy-done.3 = f32[3,384]{1,0:T(4,128)S(1)} copy-done((f32[3,384]{1,0:T(4,128)S(1)}, f32[3,384]{1,0:T(4,128)}, u32[]{:S(2)}) %copy-start.3) | copy-done | bytes 4632
  5.5 0.0 copy-start.4
  5.5 0.7 %copy-done.4 = f32[3,384]{1,0:T(4,128)S(1)} copy-done((f32[3,384]{1,0:T(4,128)S(1)}, f32[3,384]{1,0:T(4,128)}, u32[]{:S(2)}) %copy-start.4) | copy-done | bytes 4632
  6.2 0.0 copy-start.5
  6.2 0.7 copy-done.5
  6.8 57.8 %ewald.1 = f32[8,384]{1,0:T(8,128)S(1)} custom-call(s32[3,384]{1,0:T(4,128)S(1)} %copy-done.2, f32[3,384]{1,0:T(4,128)S(1)} %copy-done.3, f32[1,384]{1,0:T(1,128)S(1)} %reshape.11.charge_ref, f32[3,384]{1,0:T(4,128)S(1)} %copy-done.4, s32[6]{0:T(128)S(1)} %copy-done.5, s32[1]{0:T(128)S(6)} %copy.15.shear_ref, bf16[768,384]{1,0:T(8,128)(2,1)S(1)} %copy-done, ...), custom_call_target="tpu_custom_call" | custom-call | tf_op jit(solution)/shard_map/ewald/pallas_call | solution.py:663
  64.6 0.6 fusion
  65.3 0.6 slice_reduce_fusion
  65.8 0.5 slice.15
Async XLA Ops:
  2.0 1.1 %copy-start = (bf16[768,384]{1,0:T(8,128)(2,1)S(1)}, bf16[768,384]{1,0:T(8,128)(2,1)}, u32[]{:S(2)}) copy-start(bf16[768,384]{1,0:T(8,128)(2,1)} %constant.10.clone.cf_high_hbm) | copy-start | bytes 1769476
  3.0 1.1 %copy-start.1 = (bf16[768,384]{1,0:T(8,128)(2,1)S(1)}, bf16[768,384]{1,0:T(8,128)(2,1)}, u32[]{:S(2)}) copy-start(bf16[768,384]{1,0:T(8,128)(2,1)} %constant.11.clone.cf_low_hbm) | copy-start | bytes 1769476
  4.1 0.7 %copy-start.2 = (s32[3,384]{1,0:T(4,128)S(1)}, s32[3,384]{1,0:T(4,128)}, u32[]{:S(2)}) copy-start(s32[3,384]{1,0:T(4,128)} %cell_ref.1) | copy-start | bytes 13828
  4.8 0.7 %copy-start.3 = (f32[3,384]{1,0:T(4,128)S(1)}, f32[3,384]{1,0:T(4,128)}, u32[]{:S(2)}) copy-start(f32[3,384]{1,0:T(4,128)} %off_ref.1) | copy-start | bytes 13828
  5.5 0.7 %copy-start.4 = (f32[3,384]{1,0:T(4,128)S(1)}, f32[3,384]{1,0:T(4,128)}, u32[]{:S(2)}) copy-start(f32[3,384]{1,0:T(4,128)} %dip_ref.1) | copy-start | bytes 13828
  6.2 0.7 copy-start.5

commit v2 on v1

--- a/solution.py
+++ b/solution.py
@@ -14,6 +14,7 @@
 NZ = 360
 CY = 6
 LANES = 128
+ROWS = 2 * CY - 1
 UNIT_X = 32
 WIN = 40
 EXT = NX + 8
@@ -21,7 +22,7 @@
 MESH = pl.DeviceIdType.MESH
 F32 = jnp.float32
 BF16 = jnp.bfloat16
-VMEM_LIMIT = 52 * 1024 * 1024
+VMEM_LIMIT = 63 * 1024 * 1024
 
 
 def spline_tables(fraction):
@@ -237,20 +238,35 @@
 
 def whole_kernel(
     groups, pencils, per_pencil, blocks, kz_part, kzt, kzp, rows_pad,
-    cell_ref, off_ref, charge_ref, dip_ref, count_ref, shear_ref,
+    cell_hbm, off_hbm, charge_hbm, dip_hbm, count_hbm, shear_hbm,
     cf_high_hbm, cf_low_hbm, c_hbm, w1_hbm, w2_hbm,
     out_ref,
+    cell_ref, off_ref, charge_ref, dip_ref, count_ref, shear_ref,
     cf_high, cf_low, c_both, w1_both, w2_both,
     own, gathered, weights, z_high, z_low, cells, lhs, rhs_high, rhs_low,
     send, arrived, filtered, back, gtab_ref, phase_ref, step_ref, shares, parts, held,
-    const_sem, get_send, get_recv, out_send, out_recv, back_send, back_recv,
+    input_sem, const_sem, get_send, get_recv, out_send, out_recv, back_send, back_recv,
     told_send, told_recv, ret_send, ret_recv,
 ):
     g, s = my_group(groups, pencils)
     ny = CY * groups
     zr = 2 * kzt
     modes = ny * kzp
-    shear = shear_ref[0]
+    inputs = [
+        pltpu.make_async_copy(source, target, input_sem.at[i])
+        for i, (source, target) in enumerate(
+            [
+                (cell_hbm, cell_ref),
+                (off_hbm, off_ref),
+                (charge_hbm, charge_ref),
+                (dip_hbm, dip_ref),
+                (count_hbm, count_ref),
+                (shear_hbm, shear_ref),
+            ]
+        )
+    ]
+    for load in inputs:
+        load.start()
     targets = ring_targets(groups, pencils, g, s)
     sources = ring_sources(groups, pencils, g, s)
     peers = [lax.rem(s + k, groups) for k in range(1, groups)]
@@ -280,23 +296,28 @@
     for load in loads:
         load.start()
 
-    atoms = own.shape[1]
+    for load in inputs:
+        load.wait()
+    shear = shear_ref[0]
+    atoms = out_ref.shape[1]
     per_block = atoms // blocks
     lane = lax.broadcasted_iota(jnp.int32, (1, atoms), 1)
     live = jnp.zeros((1, atoms), F32)
     for b in range(blocks):
         first = b * per_block
         live = jnp.where((lane >= first) & (lane < first + count_ref[b]), 1.0, live)
-    own[...] = jnp.concatenate(
+    told_rows = jnp.concatenate(
         [
             cell_ref[...].astype(F32),
             off_ref[...],
-            charge_ref[...] * live,
+            charge_ref[...].reshape(1, atoms) * live,
             dip_ref[...] * live,
-            jnp.zeros((6, atoms), F32),
         ],
         axis=0,
     )
+    own[...] = jnp.zeros_like(own)
+    for k in range(per_pencil):
+        own[k * 10 : (k + 1) * 10] = told_rows[:, k * LANES : (k + 1) * LANES]
     pl.semaphore_wait(barrier, len(sources) + len(targets) + len(peers))
 
     def get_copy(i, pg, ps, slot):
@@ -333,29 +354,37 @@
         for p in range(groups):
             send[p, used:rows_pad] = jnp.zeros((rows_pad - used, NX), F32)
 
-    for pg, ps, slot in sources:
-        here = (pg == g) & (ps == s)
-
-        @pl.when(jnp.logical_not(here))
-        def _():
-            get_copy(0, pg, ps, slot).wait_recv()
+    def source_of(v, j):
+        flat = lax.rem(s - v + groups, groups) * pencils + j
+        pg, ps = flat // groups, lax.rem(flat, groups)
+        return pg, ps, (pg == g) & (ps == s)
 
     slab_low = lax.rem(s - 1 + groups, groups)
     y_base = [(s * CY).astype(F32), (slab_low * CY + CY).astype(F32)]
 
     def spread(j, carry):
+        for v in range(2):
+            pg, ps, here = source_of(v, j)
+
+            @pl.when(jnp.logical_not(here))
+            def _():
+                get_copy(0, pg, ps, v * pencils + j).wait_recv()
+
         for k in range(per_pencil):
             x_at = pl.multiple_of((j * per_pencil + k) * UNIT_X, UNIT_X)
             x_base = x_at.astype(F32)
             for v in range(2):
                 unit = (j * 2 + v) * per_pencil + k
-                atom = gathered[v * pencils + j, :, k * LANES : (k + 1) * LANES]
+                atom = gathered[v * pencils + j, k * 10 : (k + 1) * 10]
                 tables = spline_tables(atom[3:6])
                 wx = dense_rows(tables, 0, atom[0:1] - x_base, WIN)
                 wy = dense_rows(tables, 1, atom[1:2] - y_base[v], 8)
                 z0, z1, z2 = mode_weights(tables, atom[2:3], kz, step_ref)
                 weights[unit] = jnp.concatenate(wx + wy, axis=0)
-                high, low = split(jnp.concatenate([z0, z1, z2], axis=1))
+                z_all = [jnp.concatenate([z0, z1, z2], axis=1)]
+                if zr < LANES:
+                    z_all.append(jnp.zeros((LANES - zr, 3 * LANES), F32))
+                high, low = split(jnp.concatenate(z_all, axis=0))
                 z_high[unit] = high
                 z_low[unit] = low
                 q, mx, my, mz = (atom[i : i + 1] for i in range(6, 10))
@@ -371,20 +400,20 @@
                             ],
                             axis=1,
                         )
-                        for y in range(CY)
+                        for y in range(CY - v)
                     ],
                     axis=0,
                 )
                 part = dot3(stacked(left), *split(right), NT)
-                for y in range(CY):
+                for y in range(CY - v):
                     here = cells.at[v * CY + y, pl.ds(x_at, WIN), pl.ds(0, zr)]
                     here[...] = here[...] + part[y * WIN : (y + 1) * WIN]
         return carry
 
     lax.fori_loop(0, pencils, spread, 0)
 
-    total = 2 * CY * zr
-    for at in range(2 * CY):
+    total = ROWS * zr
+    for at in range(ROWS):
         cells[at, 0:8] = cells[at, 0:8] + cells[at, NX:EXT]
         turned = jnp.transpose(cells[at, 0:NX])
         cos_part, sin_part = turned[0:kzt], turned[kzt:zr]
@@ -422,7 +451,7 @@
         lines = dot3(lhs[...], cf_high[:, cols], cf_low[:, cols], NN)
         for y in range(CY):
             real, imag = 0.0, 0.0
-            for v in range(2):
+            for v in range(2 if y < CY - 1 else 1):
                 at = v * CY + y
                 ct, st = phase_ref[0, at : at + 1, cols], phase_ref[1, at : at + 1, cols]
                 re = lines[at * zr : at * zr + kzt]
@@ -495,7 +524,7 @@
                     )
                 )
             real, imag = found
-            for v in range(2):
+            for v in range(2 if y < CY - 1 else 1):
                 at = v * CY + y
                 ct, st = phase_ref[0, at : at + 1, cols], phase_ref[1, at : at + 1, cols]
                 pr = real * ct - imag * st
@@ -509,19 +538,15 @@
                 high, low = split(jnp.concatenate(rows, axis=0))
                 rhs_high[at * LANES : (at + 1) * LANES, deep] = high
                 rhs_low[at * LANES : (at + 1) * LANES, deep] = low
-        for pair in range(CY):
-            at = pair * 2 * LANES
-            found = dot3(
-                c_both[:, deep],
-                rhs_high[at : at + 2 * LANES, deep],
-                rhs_low[at : at + 2 * LANES, deep],
-                NT,
-            )
-            for half in range(2):
-                here = cells.at[2 * pair + half, 0:NX]
+        for pair in range(0, ROWS, 2):
+            many = min(2, ROWS - pair)
+            at = slice(pair * LANES, (pair + many) * LANES)
+            found = dot3(c_both[:, deep], rhs_high[at, deep], rhs_low[at, deep], NT)
+            for half in range(many):
+                here = cells.at[pair + half, 0:NX]
                 part = found[:, half * LANES : (half + 1) * LANES]
                 here[...] = part if chunk == 0 else here[...] + part
-    for at in range(2 * CY):
+    for at in range(ROWS):
         cells[at, NX:EXT] = cells[at, 0:8]
 
     for copy in told:
@@ -546,10 +571,15 @@
                 unit = (j * 2 + v) * per_pencil + k
                 slot = v * pencils + j
                 left = jnp.concatenate(
-                    [cells[v * CY + y, pl.ds(x_at, WIN), pl.ds(0, zr)] for y in range(CY)],
-                    axis=0,
+                    [cells[v * CY + y, pl.ds(x_at, WIN)] for y in range(CY - v)], axis=0
                 )
-                proj = dot3(stacked(left), z_high[unit], z_low[unit], NN)
+                high, low = split(left)
+                z_now = z_high[unit]
+                proj = dot(
+                    jnp.concatenate([high, low], axis=1),
+                    jnp.concatenate([z_now, z_now], axis=0),
+                    NN,
+                ) + dot(high, z_low[unit], NN)
                 wx = [weights[unit, o * WIN : (o + 1) * WIN] for o in range(3)]
                 wy = [weights[unit, 3 * WIN + o * 8 : 3 * WIN + (o + 1) * 8] for o in range(3)]
 
@@ -557,7 +587,7 @@
                     return sum(
                         wy[r][y : y + 1]
                         * proj[y * WIN : (y + 1) * WIN, order * LANES : (order + 1) * LANES]
-                        for y in range(CY)
+                        for y in range(CY - v)
                     )
 
                 def over_x(p, values):
@@ -570,7 +600,7 @@
                 s020 = over_x(0, over_y(2, 0))
                 s002 = over_x(0, over_y(0, 2))
                 s011 = over_x(0, over_y(1, 1))
-                atom = gathered[slot, :, k * LANES : (k + 1) * LANES]
+                atom = gathered[slot, k * 10 : (k + 1) * 10]
                 q, mx, my, mz = (atom[i : i + 1] for i in range(6, 10))
                 parts[slot, :, k * LANES : (k + 1) * LANES] = jnp.concatenate(
                     [
@@ -585,21 +615,21 @@
                     ],
                     axis=0,
                 )
+        for v in range(2):
+            slot, to_slot = v * pencils + j, v * pencils + g
+            pg, ps, here = source_of(v, j)
+
+            @pl.when(jnp.logical_not(here))
+            def _():
+                return_copy(slot, to_slot, pg, ps).start()
+
+            @pl.when(here)
+            def _():
+                held[to_slot] = parts[slot]
+
         return carry
 
     lax.fori_loop(0, pencils, sample, 0)
-
-    for i, (pg, ps, _) in enumerate(sources):
-        here = (pg == g) & (ps == s)
-        to_slot = (i // pencils) * pencils + g
-
-        @pl.when(jnp.logical_not(here))
-        def _():
-            return_copy(i, to_slot, pg, ps).start()
-
-        @pl.when(here)
-        def _():
-            held[to_slot] = parts[i]
 
     for i, (pg, ps, _) in enumerate(targets):
         here = (pg == g) & (ps == s)
@@ -644,6 +674,7 @@
     zr = 2 * kzt
     rows_pad = -(-2 * CY * kzp // 8) * 8
     slots = 2 * pencils
+    told = -(-10 * per_pencil // 8) * 8
 
     forward = x_tables()
     backward = np.concatenate(
@@ -656,7 +687,6 @@
         for table in (backward, y_table, np.ascontiguousarray(y_table.T))
     ]
     vmem = pl.BlockSpec(memory_space=pltpu.VMEM)
-    smem = pl.BlockSpec(memory_space=pltpu.SMEM)
     block = (groups, rows_pad, NX)
     peers = (groups - 1,)
     sem = pltpu.SemaphoreType.DMA
@@ -665,23 +695,29 @@
             whole_kernel, groups, pencils, per_pencil, blocks, kz_part, kzt, kzp, rows_pad
         ),
         out_shape=jax.ShapeDtypeStruct((8, atoms), F32),
-        in_specs=[vmem] * 4 + [smem] * 2 + [pl.BlockSpec(memory_space=pl.ANY)] * 5,
+        in_specs=[pl.BlockSpec(memory_space=pl.ANY)] * 11,
         out_specs=vmem,
         scratch_shapes=[
+            pltpu.VMEM(cell_index.shape, jnp.int32),
+            pltpu.VMEM(offsets.shape, F32),
+            pltpu.VMEM(charges.shape, F32),
+            pltpu.VMEM(dipoles.shape, F32),
+            pltpu.SMEM(block_count.shape, jnp.int32),
+            pltpu.SMEM(shear_cells.shape, jnp.int32),
             pltpu.VMEM((2 * NX, NX), BF16),
             pltpu.VMEM((2 * NX, NX), BF16),
             pltpu.VMEM((2 * NX, 2 * NX), BF16),
             pltpu.VMEM((4 * ny * kzp, groups * rows_pad), BF16),
             pltpu.VMEM((2 * groups * rows_pad, 2 * ny * kzp), BF16),
-            pltpu.VMEM((16, atoms), F32),
-            pltpu.VMEM((slots, 16, atoms), F32),
+            pltpu.VMEM((told, LANES), F32),
+            pltpu.VMEM((slots, told, LANES), F32),
             pltpu.VMEM((2 * units, 3 * WIN + 24, LANES), F32),
-            pltpu.VMEM((2 * units, zr, 3 * LANES), BF16),
-            pltpu.VMEM((2 * units, zr, 3 * LANES), BF16),
-            pltpu.VMEM((2 * CY, EXT, LANES), F32),
-            pltpu.VMEM((4 * CY * zr, 2 * NX), BF16),
-            pltpu.VMEM((2 * CY * LANES, 2 * NX), BF16),
-            pltpu.VMEM((2 * CY * LANES, 2 * NX), BF16),
+            pltpu.VMEM((2 * units, LANES, 3 * LANES), BF16),
+            pltpu.VMEM((2 * units, LANES, 3 * LANES), BF16),
+            pltpu.VMEM((ROWS, EXT, LANES), F32),
+            pltpu.VMEM((2 * ROWS * zr, 2 * NX), BF16),
+            pltpu.VMEM((ROWS * LANES, 2 * NX), BF16),
+            pltpu.VMEM((ROWS * LANES, 2 * NX), BF16),
             pltpu.VMEM(block, F32),
             pltpu.VMEM(block, F32),
             pltpu.VMEM(block, F32),
@@ -692,6 +728,7 @@
             pltpu.VMEM((groups, 8, LANES), F32),
             pltpu.VMEM((slots, 8, atoms), F32),
             pltpu.VMEM((slots, 8, atoms), F32),
+            sem((6,)),
             sem((5,)),
             sem((slots,)),
             sem((slots,)),
@@ -711,7 +748,7 @@
     )(
         cell_index,
         offsets,
-        charges.reshape(1, atoms),
+        charges,
         dipoles,
         block_count,
         shear_cells,

time: 67.7 us -> 59.2 us (0.87); the launches traced: 66.4 us -> 58.8 us
  Pallas kernels: 57.8 us -> 53.6 us
  local copies, waits for them, and re-layouts: 7.25 us -> 3.88 us
    unnamed x12 -> x0, local copies, waits for them, and re-layouts: 4.85 us -> none
    pallas_call x1, Pallas kernels: 57.8 us -> 53.6 us  [on_device(): pl.pallas_call(functools.partial(whole_kernel, groups, pencils, per_penci...]
    slice x3, local copies, waits for them, and re-layouts: 1.71 us -> 3.88 us  [on_device(): return (result[0], result[1:4], result[4:7], result[7, 0:1])]
    reshape x1 -> x0, local copies, waits for them, and re-layouts: 0.68 us -> none  [on_device(): charges.reshape(1, atoms)]
where the time goes in v2:
time: 59.2 us; the launch traced here: 58.8 us
  Pallas kernels  53.6 us (91%)
  local copies, waits for them, and re-layouts  3.88 us (7%)
  between operations  1.29 us (2%)
    pallas_call x1, Pallas kernels, on_device(): pl.pallas_call(functools.partial(whole_kernel, groups, pencils, per_penci...  53.6 us
    slice x3, local copies, waits for them, and re-layouts, on_device(): return (result[0], result[1:4], result[4:7], result[7, 0:1])  3.88 us

profile of v2, /device:TPU:5, one launch (start us, length us, event | category | flops | bytes accessed | tf_op | source)
XLA Modules:
  0.0 58.8 jit_solution(8443994421552925577)
XLA Ops:
  1.3 53.6 %ewald.1 = f32[8,384]{1,0:T(8,128)} custom-call(s32[3,384]{1,0:T(4,128)} %cell_hbm.1, f32[3,384]{1,0:T(4,128)} %off_hbm.1, f32[384]{0:T(512)} %charge_hbm.1, f32[3,384]{1,0:T(4,128)} %dip_hbm.1, s32[6]{0:T(128)} %count_hbm.1, s32[1]{0:T(128)S(6)} %copy.15.shear_hbm, bf16[768,384]{1,0:T(8,128)(2,1)} %constant.10.clone.cf_high_hbm, ...), custom_call_target="tpu_custom_call" | custom-call | tf_op jit(solution)/shard_map/ewald/pallas_call | solution.py:693
  54.9 1.4 %fusion = (f32[3,384]{1,0:T(4,128)}, f32[3,384]{1,0:T(4,128)}) fusion(f32[8,384]{1,0:T(8,128)} %ewald.1), kind=kLoop, calls=%fused_computation.1 | loop fusion | bytes 18432 | tf_op jit(solution)/shard_map/slice | solution.py:760
  56.3 1.3 %slice_reduce_fusion = f32[384]{0:T(512)} fusion(f32[8,384]{1,0:T(8,128)} %ewald.1), kind=kLoop, calls=%fused_computation | loop fusion | bytes 3072 | tf_op jit(solution)/shard_map/slice | solution.py:760
  57.6 1.2 %slice.15 = f32[1,1]{1,0:T(1,128)} slice(f32[8,384]{1,0:T(8,128)} %ewald.1), slice={[7:8], [0:1]} | slice | bytes 8 | tf_op jit(solution)/shard_map/slice | solution.py:760

commit v3 on v2

--- a/solution.py
+++ b/solution.py
@@ -76,6 +76,12 @@
     m = left.shape[0] // 2
     both = dot(left, right_high, dims)
     return both[:m] + (both[m:] + dot(left[:m], right_low, dims))
+
+
+def dot_wide(left, right_high, right_low, dims):
+    k = left.shape[1] // 2
+    twice = jnp.concatenate([right_high, right_high], axis=0)
+    return dot(left, twice, dims) + dot(left[:, :k], right_low, dims)
 
 
 def stacked(x):
@@ -412,7 +418,6 @@
 
     lax.fori_loop(0, pencils, spread, 0)
 
-    total = ROWS * zr
     for at in range(ROWS):
         cells[at, 0:8] = cells[at, 0:8] + cells[at, NX:EXT]
         turned = jnp.transpose(cells[at, 0:NX])
@@ -426,8 +431,8 @@
                 axis=0,
             )
         )
-        lhs[at * zr : (at + 1) * zr] = high
-        lhs[total + at * zr : total + (at + 1) * zr] = low
+        lhs[at * zr : (at + 1) * zr, 0 : 2 * NX] = high
+        lhs[at * zr : (at + 1) * zr, 2 * NX : 4 * NX] = low
 
     def chunk_copies(source, target, send_sems, recv_sems, chunk):
         first, count = CHUNKS[chunk]
@@ -448,7 +453,7 @@
     sent = []
     for chunk, (first, count) in enumerate(CHUNKS):
         cols = slice(first, first + count)
-        lines = dot3(lhs[...], cf_high[:, cols], cf_low[:, cols], NN)
+        lines = dot_wide(lhs[...], cf_high[:, cols], cf_low[:, cols], NN)
         for y in range(CY):
             real, imag = 0.0, 0.0
             for v in range(2 if y < CY - 1 else 1):
@@ -478,7 +483,7 @@
         for copy in sent[chunk]:
             copy.wait_recv()
         high, low = split(arrived[:, :, cols].reshape(flat, count))
-        spectrum = dot3(w1_both[...], high, low, NN)
+        spectrum = dot_wide(w1_both[...], high, low, NN)
         real, imag = spectrum[:modes], spectrum[modes:]
         gtab = gtab_ref[:, cols]
         amount = jnp.sum(
@@ -487,7 +492,7 @@
         for i in range(0, count, LANES):
             power = power + amount[:, i : i + LANES]
         high, low = split(jnp.concatenate([gtab * real, gtab * imag], axis=0))
-        filtered[:, :, cols] = dot3(w2_both[...], high, low, NN).reshape(groups, rows_pad, count)
+        filtered[:, :, cols] = dot_wide(w2_both[...], high, low, NN).reshape(groups, rows_pad, count)
         copies = chunk_copies(filtered, back, back_send, back_recv, chunk)
         for copy in copies:
             copy.start()
@@ -662,6 +667,13 @@
             return_copy(i, 0, pg, ps).wait_send()
 
 
+def part_kernel(rows_ref, charge_ref, dipole_ref, position_ref, energy_ref):
+    charge_ref[...] = rows_ref[0:1].reshape(charge_ref.shape)
+    dipole_ref[...] = rows_ref[1:4]
+    position_ref[...] = rows_ref[4:7]
+    energy_ref[...] = rows_ref[7:8, 0:1]
+
+
 def on_device(groups, pencils, cell_index, offsets, charges, dipoles, block_count, shear_cells):
     atoms = charges.shape[0]
     blocks = block_count.shape[0]
@@ -682,9 +694,9 @@
     )
     y_table = y_tables(groups, kzp, rows_pad)
     cf_high, cf_low = split_np(forward)
-    constants = [cf_high, cf_low] + [
-        np.concatenate(split_np(table), axis=0)
-        for table in (backward, y_table, np.ascontiguousarray(y_table.T))
+    constants = [cf_high, cf_low, np.concatenate(split_np(backward), axis=0)] + [
+        np.concatenate(split_np(table), axis=1)
+        for table in (y_table, np.ascontiguousarray(y_table.T))
     ]
     vmem = pl.BlockSpec(memory_space=pltpu.VMEM)
     block = (groups, rows_pad, NX)
@@ -707,15 +719,15 @@
             pltpu.VMEM((2 * NX, NX), BF16),
             pltpu.VMEM((2 * NX, NX), BF16),
             pltpu.VMEM((2 * NX, 2 * NX), BF16),
-            pltpu.VMEM((4 * ny * kzp, groups * rows_pad), BF16),
-            pltpu.VMEM((2 * groups * rows_pad, 2 * ny * kzp), BF16),
+            pltpu.VMEM((2 * ny * kzp, 2 * groups * rows_pad), BF16),
+            pltpu.VMEM((groups * rows_pad, 4 * ny * kzp), BF16),
             pltpu.VMEM((told, LANES), F32),
             pltpu.VMEM((slots, told, LANES), F32),
             pltpu.VMEM((2 * units, 3 * WIN + 24, LANES), F32),
             pltpu.VMEM((2 * units, LANES, 3 * LANES), BF16),
             pltpu.VMEM((2 * units, LANES, 3 * LANES), BF16),
             pltpu.VMEM((ROWS, EXT, LANES), F32),
-            pltpu.VMEM((2 * ROWS * zr, 2 * NX), BF16),
+            pltpu.VMEM((ROWS * zr, 4 * NX), BF16),
             pltpu.VMEM((ROWS * LANES, 2 * NX), BF16),
             pltpu.VMEM((ROWS * LANES, 2 * NX), BF16),
             pltpu.VMEM(block, F32),
@@ -757,7 +769,19 @@
             for t in (constants[0], constants[1], constants[2], constants[3], constants[4])
         ],
     )
-    return result[0], result[1:4], result[4:7], result[7, 0:1]
+    charge_grad, dipole_grad, position_grad, energy = pl.pallas_call(
+        part_kernel,
+        out_shape=(
+            jax.ShapeDtypeStruct((atoms,), F32),
+            jax.ShapeDtypeStruct((3, atoms), F32),
+            jax.ShapeDtypeStruct((3, atoms), F32),
+            jax.ShapeDtypeStruct((1, 1), F32),
+        ),
+        in_specs=[vmem],
+        out_specs=(vmem,) * 4,
+        name="part_outputs",
+    )(result)
+    return charge_grad, dipole_grad, position_grad, energy.reshape(1)
 
 
 def solution(mesh):

time: 59.2 us -> 56.2 us (0.949)
  local copies, waits for them, and re-layouts: 3.88 us -> 0 us
  Pallas kernels: 53.6 us -> 54.7 us
    slice x3 -> x0, local copies, waits for them, and re-layouts: 3.88 us -> none  [on_device(): return (result[0], result[1:4], result[4:7], result[7, 0:1])]
    pallas_call x0 -> x1, Pallas kernels: none -> 1.32 us  [on_device(): pl.pallas_call(part_kernel, out_shape=(jax.ShapeDtypeStruct((atoms,), F32...]
where the time goes in v3:
time: 56.2 us; the launch traced here: 56 us
  Pallas kernels  54.7 us (97%)
  between operations  1.29 us (2%)
    pallas_call x1, Pallas kernels, on_device(): pl.pallas_call(functools.partial(whole_kernel, groups, pencils, per_penci...  53.4 us
    pallas_call x1, Pallas kernels, on_device(): pl.pallas_call(part_kernel, out_shape=(jax.ShapeDtypeStruct((atoms,), F32...  1.32 us

profile of v3, /device:TPU:5, one launch (start us, length us, event | category | flops | bytes accessed | tf_op | source)
XLA Modules:
  0.0 56.0 jit_solution(5057354270794614204)
XLA Ops:
  1.3 53.4 %ewald.1.rows_ref = f32[8,384]{1,0:T(8,128)} custom-call(s32[3,384]{1,0:T(4,128)} %cell_hbm.1, f32[3,384]{1,0:T(4,128)} %off_hbm.1, f32[384]{0:T(512)} %charge_hbm.1, f32[3,384]{1,0:T(4,128)} %dip_hbm.1, s32[6]{0:T(128)} %count_hbm.1, s32[1]{0:T(128)S(6)} %copy.15.shear_hbm, bf16[768,384]{1,0:T(8,128)(2,1)} %constant.10.clone.cf_high_hbm, ...), custom_call_target="tpu_custom_call" | custom-call | tf_op jit(solution)/shard_map/ewald/pallas_call | solution.py:705
  54.7 1.3 %part_outputs.1 = (f32[384]{0:T(512)}, f32[3,384]{1,0:T(4,128)}, f32[3,384]{1,0:T(4,128)}, f32[1,1]{1,0:T(1,128)}) custom-call(f32[8,384]{1,0:T(8,128)} %ewald.1.rows_ref), custom_call_target="tpu_custom_call" | custom-call | tf_op jit(solution)/shard_map/part_outputs/pallas_call | solution.py:772
